TPU v7x, 32 devices: a whole 2x2x4 slice. The times are simulated.
32 devices in a mesh: dp: 4 (over y, x), expert: 8 (over z, core).
Axes of the slice: x: 2, y: 2, z: 4, core: 2. Of those that a mesh axis runs over, the one named last changes fastest.
Arguments:
- output_grad: bfloat16 [6144, 2048], P(('dp', 'expert')), may hold values from -3 to 3
- routes: int32 [6144, 2], P(('dp', 'expert')), may hold values from 0 to 7, all different within a row; in each aligned block of 192 rows (0 to 191, 192 to 383, ...) at most 72 rows name the same one
- combine_weights: bfloat16 [6144, 2], P(('dp', 'expert')), may hold values from 0.049804688 to 0.5
- saved_hidden: bfloat16 [18432, 768], P(('dp', 'expert')), may hold values from -0.796875 to 0.796875
- down_weight: bfloat16 [8, 768, 2048], P('expert', 'dp'), may hold values from -0.21875 to 0.21875
Outputs:
- hidden_grad: bfloat16 [18432, 768], P(('dp', 'expert'))
- weight_grad: float32 [8, 768, 2048], P('expert', 'dp')
- route_grad: float32 [6144, 2], P(('dp', 'expert'))
Inputs may be any that keep to these rules, and one draw needn't show every extreme that they name: Each token names 2 different experts; among the 192 rows of one device no expert is named by more than 72 routes.
All inputs are finite; a program needn't handle non-finite values.
Results may differ from a plain program's by a relative error of at most 0.008.
Values may be sent and summed in bfloat16 or wider, within the bound.
A program may use at most 64 MiB of HBM per device.

v0:
```python
import jax
import jax.numpy as jnp
from jax import lax
from jax.sharding import PartitionSpec as P


def route_slots(routes, experts, capacity):
    flat_ids = routes.reshape(-1)
    one_hot = (flat_ids[:, None] == jnp.arange(experts, dtype=jnp.int32)[None, :]).astype(jnp.int32)
    earlier = jnp.cumsum(one_hot, axis=0) - one_hot
    return flat_ids * capacity + jnp.sum(earlier * one_hot, axis=1)


def per_device(output_grad, routes, combine_weights, saved_hidden, down_weight):
    experts = lax.axis_size("expert")
    slot_count = saved_hidden.shape[0]
    capacity = slot_count // experts
    features = output_grad.shape[1]
    route_total = routes.shape[0] * routes.shape[1]
    target = route_slots(routes, experts, capacity)
    source = (
        jnp.full((slot_count,), route_total, jnp.int32)
        .at[target]
        .set(jnp.arange(route_total, dtype=jnp.int32))
    )
    is_live = source < route_total
    safe_index = jnp.where(is_live, source, 0)
    send_rows = jnp.where(
        is_live[:, None], output_grad[safe_index // routes.shape[1]], jnp.zeros((), jnp.bfloat16)
    )
    send_weights = jnp.where(
        is_live, combine_weights.reshape(-1)[safe_index], jnp.zeros((), jnp.bfloat16)
    )
    recv_rows, recv_weights = (
        lax.all_to_all(
            send_rows.reshape(experts, capacity, features),
            "expert",
            split_axis=0,
            concat_axis=0,
            tiled=True,
        ),
        lax.all_to_all(
            send_weights.reshape(experts, capacity),
            "expert",
            split_axis=0,
            concat_axis=0,
            tiled=True,
        ),
    )
    grad_rows = recv_rows.reshape(slot_count, features)
    slot_weights = recv_weights.reshape(slot_count).astype(jnp.float32)
    weighted = (slot_weights[:, None] * grad_rows.astype(jnp.float32)).astype(jnp.bfloat16)
    weight_shard = down_weight[0]
    contract = (((1,), (1,)), ((), ()))
    full_weight = lax.all_gather(weight_shard, "dp", axis=0, tiled=True)
    unscaled = lax.dot_general(grad_rows, full_weight, contract, preferred_element_type=jnp.float32)
    route_terms = jnp.sum(saved_hidden.astype(jnp.float32) * unscaled, axis=1)
    hidden_grad = (slot_weights[:, None] * unscaled).astype(jnp.bfloat16)
    grad_part = lax.psum_scatter(
        lax.dot_general(
            saved_hidden, weighted, (((0,), (0,)), ((), ())), preferred_element_type=jnp.float32
        ).astype(jnp.bfloat16),
        "dp",
        scatter_dimension=0,
        tiled=True,
    ).astype(jnp.float32)
    returned = lax.all_to_all(
        route_terms.reshape(experts, capacity), "expert", split_axis=0, concat_axis=0, tiled=True
    )
    route_grad = returned.reshape(-1)[target].reshape(routes.shape)
    return (hidden_grad, grad_part[None], route_grad)


def solution(mesh):
    return jax.shard_map(
        per_device,
        mesh=mesh,
        in_specs=(
            P(("dp", "expert"), None),
            P(("dp", "expert"), None),
            P(("dp", "expert"), None),
            P(("dp", "expert"), None),
            P("expert", "dp", None),
        ),
        out_specs=(P(("dp", "expert"), None), P("expert", "dp", None), P(("dp", "expert"), None)),
        check_vma=False,
    )
```

profile of v0, /device:TPU:0, one launch (start us, length us, event | category | flops | bytes accessed | tf_op | source)
XLA Modules:
  0.0 156.6 jit_solution(16098599032661356121)
XLA Ops:
  7.2 0.0 copy-start
  7.2 0.9 copy.16
  8.1 0.1 eq.29
  8.2 0.1 eq.25
  8.3 0.7 broadcast_multiply_fusion
  9.0 0.8 reduce-window.6
  9.9 0.2 slice_reduce_fusion
  10.1 0.1 copy.15
  10.3 0.1 mul.40
  10.4 0.1 fusion.5
  10.5 2.9 %scatter_custom_fusion = s32[576]{0:T(1024)S(1)} fusion(s32[384]{0:T(512)S(1)} %fusion.11, s32[384]{0:T(512)S(1)} %iota.11, s32[]{:T(128)} %constant.12.clone.1), kind=kCustom, calls=%fused_computation.36 | custom fusion | bytes 2308 | tf_op jit(solution)/shard_map/scatter | solution.py:24
  13.5 0.8 copy.18
  14.3 0.2 reshape.91
  14.5 3.9 %gather_fusion = bf16[576]{0:T(1024)(128)(2,1)S(1)} fusion(bf16[384]{0:T(512)(128)(2,1)S(1)} %reshape.91, s32[1024]{0:T(1024)S(1)} %pad_clamp_fusion.2), kind=kCustom, calls=%fused_computation | custom fusion | bytes 4608 | tf_op jit(solution)/shard_map/gather | solution.py:32
  18.5 0.7 all_to_all.20
  19.1 6.3 %all-to-all-start = ((bf16[8,1,72]{2,1,0:T(2,128)(2,1)}), bf16[8,1,72]{2,1,0:T(2,128)(2,1)S(1)}, u32[]{:S(2)}, u32[]{:S(2)}) async-start(bf16[8,1,72]{2,1,0:T(2,128)(2,1)} %all_to_all.20), calls=%async_computation | async-start | bytes 8192 | tf_op jit(solution)/shard_map/all_to_all | solution.py:42
  25.5 0.0 all-gather.3.cloned.1.call-start
  25.5 0.7 all-gather.3.cloned.1.call-update
  26.2 0.1 broadcast_in_dim.43
  26.3 0.0 copy-done
  26.3 3.4 %gather_fusion.1 = bf16[576,2048]{1,0:T(8,128)(2,1)S(1)} fusion(bf16[192,2048]{1,0:T(8,128)(2,1)S(1)} %copy-done, s32[1024]{0:T(1024)S(1)} %pad_clamp_fusion.1), kind=kCustom, calls=%fused_computation.1 | custom fusion | bytes 4720896 | tf_op jit(solution)/shard_map/gather | solution.py:29
  29.7 1.7 %broadcast_select_fusion = bf16[8,72,2048]{2,1,0:T(8,128)(2,1)} fusion(bf16[8,72,2048]{2,1,0:T(8,128)(2,1)S(1)} %bitcast.24, pred[8,72]{1,0:T(8,128)(4,1)S(1)} %broadcast_in_dim.43), kind=kLoop, calls=%fused_computation.10 | loop fusion | flops 1179648 | bytes 4719168 | tf_op jit(solution)/shard_map/jit(_where)/select_n | solution.py:28
  31.4 0.0 all-to-all-done
  31.4 5.1 %all-to-all-start.1 = ((bf16[8,72,2048]{2,1,0:T(8,128)(2,1)}), bf16[8,72,2048]{2,1,0:T(8,128)(2,1)S(1)}, u32[]{:S(2)}, u32[]{:S(2)}) async-start(bf16[8,72,2048]{2,1,0:T(8,128)(2,1)} %broadcast_select_fusion), calls=%async_computation.1 | async-start | bytes 4718592 | tf_op jit(solution)/shard_map/all_to_all | solution.py:35
  36.5 0.0 reduce-scatter.4.cloned.1.call-start
  36.6 0.1 reshape.95
  36.6 54.5 %all-to-all-done.1 = bf16[8,72,2048]{2,1,0:T(8,128)(2,1)S(1)} async-done(((bf16[8,72,2048]{2,1,0:T(8,128)(2,1)}), bf16[8,72,2048]{2,1,0:T(8,128)(2,1)S(1)}, u32[]{:S(2)}, u32[]{:S(2)}) %all-to-all-start.1) | async-done | bytes 2359328 | tf_op jit(solution)/shard_map/all_to_all | solution.py:35
  91.2 5.5 %fusion.2 = bf16[768,2048]{0,1:T(8,128)(2,1)} fusion(bf16[576,768]{1,0:T(8,128)(2,1)} %param.8, bf16[576,2048]{1,0:T(8,128)(2,1)S(1)} %bitcast.25, f32[576]{0:T(1024)S(1)} %reshape.95), kind=kOutput, calls=%fused_computation.8 | convolution fusion | flops 1817051136 | bytes 6392064 | tf_op jit(solution)/shard_map/dot_general | solution.py:60
  96.7 4.7 %copy.22 = bf16[768,2048]{1,0:T(8,128)(2,1)} copy(bf16[768,2048]{0,1:T(8,128)(2,1)} %fusion.2) | data formatting | bytes 6291456
  101.4 0.0 reduce-scatter.4.cloned.1.call-update
  101.4 0.0 all-gather.3.cloned.1.call-done
  101.5 5.1 %multiply_reduce_fusion = (f32[576]{0:T(1024)S(1)}, bf16[576,768]{1,0:T(8,128)(2,1)}) fusion(bf16[576,768]{1,0:T(8,128)(2,1)} %param.8, f32[576]{0:T(1024)S(1)} %reshape.95, bf16[576,2048]{1,0:T(8,128)(2,1)S(1)} %bitcast.26, bf16[1,768,2048]{2,1,0:T(8,128)(2,1)} %all-gather.3.cloned.1.call-done), kind=kOutput, calls=%fused_computation.11 | convolution fusion | flops 1814150656 | bytes 7279104 | tf_op jit(solution)/shard_map/dot_general | solution.py:56
  106.5 0.7 all_to_all.18
  107.2 3.3 %all-to-all-start.2 = ((f32[8,1,72]{2,1,0:T(1,128)}), f32[8,1,72]{2,1,0:T(1,128)S(1)}, u32[]{:S(2)}, u32[]{:S(2)}) async-start(f32[8,1,72]{2,1,0:T(1,128)} %all_to_all.18), calls=%async_computation.2 | async-start | bytes 8192 | tf_op jit(solution)/shard_map/all_to_all | solution.py:67
  110.6 5.4 %all-to-all-done.2 = f32[8,1,72]{2,1,0:T(1,128)S(1)} async-done(((f32[8,1,72]{2,1,0:T(1,128)}), f32[8,1,72]{2,1,0:T(1,128)S(1)}, u32[]{:S(2)}, u32[]{:S(2)}) %all-to-all-start.2) | async-done | bytes 2336 | tf_op jit(solution)/shard_map/all_to_all | solution.py:67
  116.0 0.5 broadcast.88
  116.5 0.7 reduce.11
  117.1 0.1 reshape.93
  117.2 1.9 %gather_fusion.2 = f32[384]{0:T(512)S(1)} fusion(f32[576]{0:T(1024)S(1)} %reshape.93, s32[1024]{0:T(1024)S(1)} %pad_clamp_fusion), kind=kCustom, calls=%fused_computation.2 | custom fusion | bytes 4608 | tf_op jit(solution)/shard_map/gather | solution.py:70
  119.1 0.1 reshape.94
  119.2 0.7 copy.21
  119.9 24.6 %reduce-scatter.4.cloned.1.call-done = bf16[192,2048]{1,0:T(8,128)(2,1)} async-done(((bf16[768,2048]{1,0:T(8,128)(2,1)}), bf16[192,2048]{1,0:T(8,128)(2,1)}) %reduce-scatter.4.cloned.1.call-update) | async-done | bytes 786448
  144.5 2.2 %copy.23 = bf16[192,2048]{0,1:T(8,128)(2,1)} copy(bf16[192,2048]{1,0:T(8,128)(2,1)} %reduce-scatter.4.cloned.1.call-done) | data formatting | bytes 1572864
  146.7 1.4 bitcast_convert_fusion
  148.1 1.7 %copy.20 = f32[1,192,2048]{2,1,0:T(8,128)} copy(f32[1,192,2048]{1,2,0:T(8,128)S(1)} %bitcast_convert_fusion) | data formatting | bytes 3145728
  (11 shorter events, 0.1 us)
Async XLA Ops:
  7.2 19.1 %copy-start = (bf16[192,2048]{1,0:T(8,128)(2,1)S(1)}, bf16[192,2048]{1,0:T(8,128)(2,1)}, u32[]{:S(2)}) copy-start(bf16[192,2048]{1,0:T(8,128)(2,1)} %param.5) | copy-start | bytes 2359300
  19.1 12.3 %all-to-all-start = ((bf16[8,1,72]{2,1,0:T(2,128)(2,1)}), bf16[8,1,72]{2,1,0:T(2,128)(2,1)S(1)}, u32[]{:S(2)}, u32[]{:S(2)}) async-start(bf16[8,1,72]{2,1,0:T(2,128)(2,1)} %all_to_all.20), calls=%async_computation | async-start | bytes 8192 | tf_op jit(solution)/shard_map/all_to_all | solution.py:42
  25.5 76.0 %all-gather.3.cloned.1.call-start = ((), (), s32[]{:S(2)}) async-start(), calls=%async_computation.4 | async-start | bytes 3932160 | tf_op jit(solution)/shard_map/all_gather | solution.py:55
  31.4 59.8 %all-to-all-start.1 = ((bf16[8,72,2048]{2,1,0:T(8,128)(2,1)}), bf16[8,72,2048]{2,1,0:T(8,128)(2,1)S(1)}, u32[]{:S(2)}, u32[]{:S(2)}) async-start(bf16[8,72,2048]{2,1,0:T(8,128)(2,1)} %broadcast_select_fusion), calls=%async_computation.1 | async-start | bytes 4718592 | tf_op jit(solution)/shard_map/all_to_all | solution.py:35
  36.5 108.0 %reduce-scatter.4.cloned.1.call-start = ((), (), s32[]{:S(2)}) async-start(), calls=%async_computation.5 | async-start | bytes 3932160
  107.2 8.7 %all-to-all-start.2 = ((f32[8,1,72]{2,1,0:T(1,128)}), f32[8,1,72]{2,1,0:T(1,128)S(1)}, u32[]{:S(2)}, u32[]{:S(2)}) async-start(f32[8,1,72]{2,1,0:T(1,128)} %all_to_all.18), calls=%async_computation.2 | async-start | bytes 8192 | tf_op jit(solution)/shard_map/all_to_all | solution.py:67
Sparse Core Ops, SparseCore 0:
  28.1 45.4 all-gather.2
  101.6 42.8 reduce-scatter.3
where the time goes:
time: 157 us
  waiting for transfers between devices  85.2 us (54%)
  local copies, waits for them, and re-layouts  26.3 us (17%)
  starting transfers between devices  14.8 us (9%)
  between operations  14.2 us (9%)
  matrix products  10.6 us (7%)
  other arithmetic  5.47 us (3%)
    all_to_all x1, waiting for transfers between devices, per_device(): lax.all_to_all(send_rows.reshape(experts, capacity, features), 'expert',...  54.5 us
    unnamed x3, waiting for transfers between devices  25.3 us
    unnamed x8, local copies, waits for them, and re-layouts  11 us
    all_to_all x1, starting transfers between devices, per_device(): lax.all_to_all(send_weights.reshape(experts, capacity), 'expert', split_a...  6.33 us
    dot_general x1, matrix products, per_device(): lax.dot_general(saved_hidden, weighted, (((0,), (0,)), ((), ())), preferr...  5.53 us
    all_to_all x1, waiting for transfers between devices, per_device(): lax.all_to_all(route_terms.reshape(experts, capacity), 'expert', split_ax...  5.4 us
    all_to_all x1, starting transfers between devices, per_device(): lax.all_to_all(send_rows.reshape(experts, capacity, features), 'expert',...  5.09 us
    dot_general x1, matrix products, per_device(): lax.dot_general(grad_rows, full_weight, contract, preferred_element_type=...  5.08 us
  transfers between devices with their start and end apart: 5, of which 3 were waited for; matrix products, arithmetic and copies ran while one was open for 16% of the time, Pallas kernels for 0%

commit v1 on v0

--- a/solution.py
+++ b/solution.py
@@ -2,6 +2,28 @@
 import jax.numpy as jnp
 from jax import lax
 from jax.sharding import PartitionSpec as P
+from jax.lax import axis_index, axis_size, ppermute
+
+
+def _supply_lanes(own_rows):
+    current_block = axis_index("expert")
+    reached = axis_size("expert")
+    state_next, known = (reached, current_block)
+    high = own_rows.shape[0] // state_next
+    passed = list(own_rows.shape)
+    passed[0] = high
+    v_next = passed[0]
+    passed[0] = v_next * state_next
+    far_arr = jnp.zeros(passed, own_rows.dtype)
+    for b in tuple(range(state_next)):
+        res = lax.dynamic_slice_in_dim(own_rows, (known ^ b) * high, high, axis=0)
+        if b:
+            blocks_here = []
+            for q in [*range(state_next)]:
+                blocks_here.append((q, q ^ b))
+            res = ppermute(res, axis_name="expert", perm=blocks_here)
+        far_arr = lax.dynamic_update_slice_in_dim(far_arr, res, (known ^ b) * v_next, axis=0)
+    return far_arr
 
 
 def route_slots(routes, experts, capacity):
@@ -39,13 +61,7 @@
             concat_axis=0,
             tiled=True,
         ),
-        lax.all_to_all(
-            send_weights.reshape(experts, capacity),
-            "expert",
-            split_axis=0,
-            concat_axis=0,
-            tiled=True,
-        ),
+        _supply_lanes(send_weights.reshape(experts, capacity)),
     )
     grad_rows = recv_rows.reshape(slot_count, features)
     slot_weights = recv_weights.reshape(slot_count).astype(jnp.float32)

time: 157 us -> 147 us (0.936)
  waiting for transfers between devices: 85.2 us -> 69.7 us
  starting transfers between devices: 14.8 us -> 21 us
    all_to_all x1, waiting for transfers between devices: 54.5 us -> 0.01 us  [per_device(): lax.all_to_all(send_rows.reshape(experts, capacity, features), 'expert',...]
    ppermute x0 -> x7, waiting for transfers between devices: none -> 39.1 us  [_supply_lanes(): res = ppermute(res, axis_name='expert', perm=blocks_here)]
    ppermute x0 -> x7, starting transfers between devices: none -> 11.1 us  [_supply_lanes(): res = ppermute(res, axis_name='expert', perm=blocks_here)]
    all_to_all x1 -> x0, starting transfers between devices: 6.33 us -> none  [per_device(): lax.all_to_all(send_weights.reshape(experts, capacity), 'expert', split_a...]
    unnamed x8 -> x10, local copies, waits for them, and re-layouts: 11 us -> 10.2 us
  transfers between devices with their start and end apart: 5 -> 11, of which waited for: 3 -> 4; matrix products, arithmetic and copies ran while one was open for 16% -> 24% of each run, Pallas kernels for 0% -> 0%
where the time goes in v1:
time: 147 us; the launch traced here: 146 us
  waiting for transfers between devices  69.7 us (47%)
  local copies, waits for them, and re-layouts  25.2 us (17%)
  starting transfers between devices  21 us (14%)
  between operations  14.3 us (10%)
  matrix products  10.6 us (7%)
  other arithmetic  5.48 us (4%)
    ppermute x7, waiting for transfers between devices, _supply_lanes(): res = ppermute(res, axis_name='expert', perm=blocks_here)  39.1 us
    unnamed x3, waiting for transfers between devices  25.3 us
    ppermute x7, starting transfers between devices, _supply_lanes(): res = ppermute(res, axis_name='expert', perm=blocks_here)  11.1 us
    unnamed x10, local copies, waits for them, and re-layouts  10.2 us
    all_to_all x1, starting transfers between devices, per_device(): lax.all_to_all(send_rows.reshape(experts, capacity, features), 'expert',...  6.46 us
    dot_general x1, matrix products, per_device(): lax.dot_general(saved_hidden, weighted, (((0,), (0,)), ((), ())), preferr...  5.53 us
    all_to_all x1, waiting for transfers between devices, per_device(): lax.all_to_all(route_terms.reshape(experts, capacity), 'expert', split_ax...  5.4 us
    dot_general x1, matrix products, per_device(): lax.dot_general(grad_rows, full_weight, contract, preferred_element_type=...  5.08 us
  transfers between devices with their start and end apart: 11, of which 4 were waited for; matrix products, arithmetic and copies ran while one was open for 24% of the time, Pallas kernels for 0%

profile of v1, /device:TPU:0, one launch (start us, length us, event | category | flops | bytes accessed | tf_op | source)
XLA Modules:
  0.0 146.3 jit_solution(6730096498077929742)
XLA Ops:
  7.2 0.0 copy-start
  7.2 0.0 all-gather.3.cloned.1.call-start
  7.2 0.7 all-gather.3.cloned.1.call-update
  7.9 0.7 broadcast_multiply_fusion
  8.6 0.8 copy.16
  9.4 0.1 eq.29
  9.5 0.1 eq.25
  9.7 0.1 copy.15
  9.8 0.1 mul.40
  10.0 0.9 reduce-window.6
  10.8 0.2 slice_reduce_fusion
  11.1 0.1 fusion.5
  11.2 2.9 %scatter_custom_fusion = s32[576]{0:T(1024)S(1)} fusion(s32[384]{0:T(512)S(1)} %fusion.11, s32[384]{0:T(512)S(1)} %iota.11, s32[]{:T(128)} %constant.18.clone.1), kind=kCustom, calls=%fused_computation.43 | custom fusion | bytes 2308 | tf_op jit(solution)/shard_map/scatter | solution.py:46
  14.2 0.1 broadcast_in_dim.47
  14.3 0.0 copy-done
  14.3 3.4 %gather_fusion.1 = bf16[576,2048]{1,0:T(8,128)(2,1)S(1)} fusion(bf16[192,2048]{1,0:T(8,128)(2,1)S(1)} %copy-done, s32[1024]{0:T(1024)S(1)} %pad_clamp_fusion.1), kind=kCustom, calls=%fused_computation.1 | custom fusion | bytes 4720896 | tf_op jit(solution)/shard_map/gather | solution.py:51
  17.7 1.7 %broadcast_select_fusion = bf16[8,72,2048]{2,1,0:T(8,128)(2,1)} fusion(bf16[8,72,2048]{2,1,0:T(8,128)(2,1)S(1)} %bitcast.24, pred[8,72]{1,0:T(8,128)(4,1)S(1)} %broadcast_in_dim.47), kind=kLoop, calls=%fused_computation.10 | loop fusion | flops 1179648 | bytes 4719168 | tf_op jit(solution)/shard_map/jit(_where)/select_n | solution.py:50
  19.4 0.0 copy-start.1
  19.4 6.5 %all-to-all-start = ((bf16[8,72,2048]{2,1,0:T(8,128)(2,1)}), bf16[8,72,2048]{2,1,0:T(8,128)(2,1)S(1)}, u32[]{:S(2)}, u32[]{:S(2)}) async-start(bf16[8,72,2048]{2,1,0:T(8,128)(2,1)} %broadcast_select_fusion), calls=%async_computation | async-start | bytes 4718592 | tf_op jit(solution)/shard_map/all_to_all | solution.py:57
  25.8 0.0 reduce-scatter.4.cloned.1.call-start
  25.9 0.0 copy-done.1
  25.9 0.1 copy.18
  26.1 0.2 reshape.89
  26.3 3.9 %gather_fusion = bf16[576]{0:T(1024)(128)(2,1)S(1)} fusion(bf16[384]{0:T(512)(128)(2,1)S(1)} %reshape.89, s32[1024]{0:T(1024)S(1)} %pad_clamp_fusion.2), kind=kCustom, calls=%fused_computation | custom fusion | bytes 4608 | tf_op jit(solution)/shard_map/gather | solution.py:54
  30.2 0.1 reshape.90
  30.3 0.5 collective-permute-start
  30.8 1.7 %collective-permute-start.1 = (bf16[1,72]{1,0:T(2,128)(2,1)S(1)}, bf16[1,72]{1,0:T(2,128)(2,1)S(1)}, u32[]{:S(2)}, u32[]{:S(2)}) collective-permute-start(bf16[1,72]{1,0:T(2,128)(2,1)S(1)} %get-tuple-element.21), channel_id=1, source_target_pairs={{0,2},{1,3},{2,0},{3,1},{4,6},{5,7},{6,4},{7,5},{8,10},{9,11},{10,... | collective-permute-start | bytes 440 | tf_op jit(solution)/shard_map/ppermute | solution.py:24
  32.5 0.0 collective-permute-start.2
  32.5 2.6 %collective-permute-start.3 = (bf16[1,72]{1,0:T(2,128)(2,1)S(1)}, bf16[1,72]{1,0:T(2,128)(2,1)S(1)}, u32[]{:S(2)}, u32[]{:S(2)}) collective-permute-start(bf16[1,72]{1,0:T(2,128)(2,1)S(1)} %get-tuple-element.19), channel_id=1, source_target_pairs={{0,4},{1,5},{2,6},{3,7},{4,0},{5,1},{6,2},{7,3},{8,12},{9,13},{10,... | collective-permute-start | bytes 440 | tf_op jit(solution)/shard_map/ppermute | solution.py:24
  35.1 0.1 collective-permute-start.4
  35.3 0.0 collective-permute-done
  35.3 3.5 %collective-permute-start.5 = (bf16[1,72]{1,0:T(2,128)(2,1)S(1)}, bf16[1,72]{1,0:T(2,128)(2,1)S(1)}, u32[]{:S(2)}, u32[]{:S(2)}) collective-permute-start(bf16[1,72]{1,0:T(2,128)(2,1)S(1)} %get-tuple-element.17), channel_id=1, source_target_pairs={{0,6},{1,7},{2,4},{3,5},{4,2},{5,3},{6,0},{7,1},{8,14},{9,15},{10,... | collective-permute-start | bytes 440 | tf_op jit(solution)/shard_map/ppermute | solution.py:24
  38.8 26.2 %collective-permute-done.1 = bf16[1,72]{1,0:T(2,128)(2,1)S(1)} collective-permute-done((bf16[1,72]{1,0:T(2,128)(2,1)S(1)}, bf16[1,72]{1,0:T(2,128)(2,1)S(1)}, u32[]{:S(2)}, u32[]{:S(2)}) %collective-permute-start.1) | collective-permute-done | bytes 176 | tf_op jit(solution)/shard_map/ppermute | solution.py:24
  65.0 2.7 %collective-permute-start.6 = (bf16[1,72]{1,0:T(2,128)(2,1)S(1)}, bf16[1,72]{1,0:T(2,128)(2,1)S(1)}, u32[]{:S(2)}, u32[]{:S(2)}) collective-permute-start(bf16[1,72]{1,0:T(2,128)(2,1)S(1)} %get-tuple-element.16), channel_id=1, source_target_pairs={{0,7},{1,6},{2,5},{3,4},{4,3},{5,2},{6,1},{7,0},{8,15},{9,14},{10,... | collective-permute-start | bytes 440 | tf_op jit(solution)/shard_map/ppermute | solution.py:24
  67.8 0.0 collective-permute-done.2
  67.8 12.8 %collective-permute-done.3 = bf16[1,72]{1,0:T(2,128)(2,1)S(1)} collective-permute-done((bf16[1,72]{1,0:T(2,128)(2,1)S(1)}, bf16[1,72]{1,0:T(2,128)(2,1)S(1)}, u32[]{:S(2)}, u32[]{:S(2)}) %collective-permute-start.3) | collective-permute-done | bytes 176 | tf_op jit(solution)/shard_map/ppermute | solution.py:24
  80.7 0.0 collective-permute-done.4
  80.7 0.0 collective-permute-done.5
  80.8 0.0 collective-permute-done.6
  80.8 0.1 reshape.94
  80.9 0.0 all-to-all-done
  80.9 5.5 %fusion.2 = bf16[768,2048]{0,1:T(8,128)(2,1)} fusion(bf16[576,768]{1,0:T(8,128)(2,1)} %param.8, bf16[576,2048]{1,0:T(8,128)(2,1)S(1)} %bitcast.25, f32[576]{0:T(1024)S(1)} %reshape.94), kind=kOutput, calls=%fused_computation.8 | convolution fusion | flops 1817051136 | bytes 6392064 | tf_op jit(solution)/shard_map/dot_general | solution.py:76
  86.4 4.7 %copy.21 = bf16[768,2048]{1,0:T(8,128)(2,1)} copy(bf16[768,2048]{0,1:T(8,128)(2,1)} %fusion.2) | data formatting | bytes 6291456
  91.1 0.0 reduce-scatter.4.cloned.1.call-update
  91.1 0.0 all-gather.3.cloned.1.call-done
  91.2 5.1 %multiply_reduce_fusion = (f32[576]{0:T(1024)S(1)}, bf16[576,768]{1,0:T(8,128)(2,1)}) fusion(bf16[576,768]{1,0:T(8,128)(2,1)} %param.8, f32[576]{0:T(1024)S(1)} %reshape.94, bf16[576,2048]{1,0:T(8,128)(2,1)S(1)} %bitcast.26, bf16[1,768,2048]{2,1,0:T(8,128)(2,1)} %all-gather.3.cloned.1.call-done), kind=kOutput, calls=%fused_computation.11 | convolution fusion | flops 1814150656 | bytes 7279104 | tf_op jit(solution)/shard_map/dot_general | solution.py:72
  96.3 0.7 all_to_all.10
  96.9 3.3 %all-to-all-start.1 = ((f32[8,1,72]{2,1,0:T(1,128)}), f32[8,1,72]{2,1,0:T(1,128)S(1)}, u32[]{:S(2)}, u32[]{:S(2)}) async-start(f32[8,1,72]{2,1,0:T(1,128)} %all_to_all.10), calls=%async_computation.1 | async-start | bytes 8192 | tf_op jit(solution)/shard_map/all_to_all | solution.py:83
  100.3 5.4 %all-to-all-done.1 = f32[8,1,72]{2,1,0:T(1,128)S(1)} async-done(((f32[8,1,72]{2,1,0:T(1,128)}), f32[8,1,72]{2,1,0:T(1,128)S(1)}, u32[]{:S(2)}, u32[]{:S(2)}) %all-to-all-start.1) | async-done | bytes 2336 | tf_op jit(solution)/shard_map/all_to_all | solution.py:83
  105.7 0.5 broadcast.89
  106.2 0.7 reduce.7
  106.9 0.1 reshape.92
  106.9 1.9 %gather_fusion.2 = f32[384]{0:T(512)S(1)} fusion(f32[576]{0:T(1024)S(1)} %reshape.92, s32[1024]{0:T(1024)S(1)} %pad_clamp_fusion), kind=kCustom, calls=%fused_computation.2 | custom fusion | bytes 4608 | tf_op jit(solution)/shard_map/gather | solution.py:86
  108.8 0.1 reshape.93
  109.0 0.7 copy.20
  109.6 24.6 %reduce-scatter.4.cloned.1.call-done = bf16[192,2048]{1,0:T(8,128)(2,1)} async-done(((bf16[768,2048]{1,0:T(8,128)(2,1)}), bf16[192,2048]{1,0:T(8,128)(2,1)}) %reduce-scatter.4.cloned.1.call-update) | async-done | bytes 786448
  134.2 2.2 %copy.22 = bf16[192,2048]{0,1:T(8,128)(2,1)} copy(bf16[192,2048]{1,0:T(8,128)(2,1)} %reduce-scatter.4.cloned.1.call-done) | data formatting | bytes 1572864
  136.4 1.4 bitcast_convert_fusion
  137.8 1.7 %copy.19 = f32[1,192,2048]{2,1,0:T(8,128)} copy(f32[1,192,2048]{1,2,0:T(8,128)S(1)} %bitcast_convert_fusion) | data formatting | bytes 3145728
  (20 shorter events, 0.4 us)
Async XLA Ops:
  7.2 7.1 %copy-start = (bf16[192,2048]{1,0:T(8,128)(2,1)S(1)}, bf16[192,2048]{1,0:T(8,128)(2,1)}, u32[]{:S(2)}) copy-start(bf16[192,2048]{1,0:T(8,128)(2,1)} %param.5) | copy-start | bytes 2359300
  7.2 84.0 %all-gather.3.cloned.1.call-start = ((), (), s32[]{:S(2)}) async-start(), calls=%async_computation.3 | async-start | bytes 3932160 | tf_op jit(solution)/shard_map/all_gather | solution.py:71
  19.4 6.5 %copy-start.1 = (bf16[192,2]{0,1:T(2,128)(2,1)S(1)}, bf16[192,2]{0,1:T(2,128)(2,1)}, u32[]{:S(2)}) copy-start(bf16[192,2]{0,1:T(2,128)(2,1)} %param.7) | copy-start | bytes 2308
  19.4 61.5 %all-to-all-start = ((bf16[8,72,2048]{2,1,0:T(8,128)(2,1)}), bf16[8,72,2048]{2,1,0:T(8,128)(2,1)S(1)}, u32[]{:S(2)}, u32[]{:S(2)}) async-start(bf16[8,72,2048]{2,1,0:T(8,128)(2,1)} %broadcast_select_fusion), calls=%async_computation | async-start | bytes 4718592 | tf_op jit(solution)/shard_map/all_to_all | solution.py:57
  25.8 108.3 %reduce-scatter.4.cloned.1.call-start = ((), (), s32[]{:S(2)}) async-start(), calls=%async_computation.4 | async-start | bytes 3932160
  30.3 4.9 %collective-permute-start = (bf16[1,72]{1,0:T(2,128)(2,1)S(1)}, bf16[1,72]{1,0:T(2,128)(2,1)S(1)}, u32[]{:S(2)}, u32[]{:S(2)}) collective-permute-start(bf16[1,72]{1,0:T(2,128)(2,1)S(1)} %get-tuple-element.22), channel_id=1, source_target_pairs={{0,1},{1,0},{2,3},{3,2},{4,5},{5,4},{6,7},{7,6},{8,9},{9,8},{10,11... | collective-permute-start | bytes 440 | tf_op jit(solution)/shard_map/ppermute | solution.py:24
  30.8 34.2 %collective-permute-start.1 = (bf16[1,72]{1,0:T(2,128)(2,1)S(1)}, bf16[1,72]{1,0:T(2,128)(2,1)S(1)}, u32[]{:S(2)}, u32[]{:S(2)}) collective-permute-start(bf16[1,72]{1,0:T(2,128)(2,1)S(1)} %get-tuple-element.21), channel_id=1, source_target_pairs={{0,2},{1,3},{2,0},{3,1},{4,6},{5,7},{6,4},{7,5},{8,10},{9,11},{10,... | collective-permute-start | bytes 440 | tf_op jit(solution)/shard_map/ppermute | solution.py:24
  32.5 35.3 %collective-permute-start.2 = (bf16[1,72]{1,0:T(2,128)(2,1)S(1)}, bf16[1,72]{1,0:T(2,128)(2,1)S(1)}, u32[]{:S(2)}, u32[]{:S(2)}) collective-permute-start(bf16[1,72]{1,0:T(2,128)(2,1)S(1)} %get-tuple-element.20), channel_id=1, source_target_pairs={{0,3},{1,2},{2,1},{3,0},{4,7},{5,6},{6,5},{7,4},{8,11},{9,10},{10,... | collective-permute-start | bytes 440 | tf_op jit(solution)/shard_map/ppermute | solution.py:24
  32.5 48.1 %collective-permute-start.3 = (bf16[1,72]{1,0:T(2,128)(2,1)S(1)}, bf16[1,72]{1,0:T(2,128)(2,1)S(1)}, u32[]{:S(2)}, u32[]{:S(2)}) collective-permute-start(bf16[1,72]{1,0:T(2,128)(2,1)S(1)} %get-tuple-element.19), channel_id=1, source_target_pairs={{0,4},{1,5},{2,6},{3,7},{4,0},{5,1},{6,2},{7,3},{8,12},{9,13},{10,... | collective-permute-start | bytes 440 | tf_op jit(solution)/shard_map/ppermute | solution.py:24
  35.1 45.6 %collective-permute-start.4 = (bf16[1,72]{1,0:T(2,128)(2,1)S(1)}, bf16[1,72]{1,0:T(2,128)(2,1)S(1)}, u32[]{:S(2)}, u32[]{:S(2)}) collective-permute-start(bf16[1,72]{1,0:T(2,128)(2,1)S(1)} %get-tuple-element.18), channel_id=1, source_target_pairs={{0,5},{1,4},{2,7},{3,6},{4,1},{5,0},{6,3},{7,2},{8,13},{9,12},{10,... | collective-permute-start | bytes 440 | tf_op jit(solution)/shard_map/ppermute | solution.py:24
  35.3 45.5 %collective-permute-start.5 = (bf16[1,72]{1,0:T(2,128)(2,1)S(1)}, bf16[1,72]{1,0:T(2,128)(2,1)S(1)}, u32[]{:S(2)}, u32[]{:S(2)}) collective-permute-start(bf16[1,72]{1,0:T(2,128)(2,1)S(1)} %get-tuple-element.17), channel_id=1, source_target_pairs={{0,6},{1,7},{2,4},{3,5},{4,2},{5,3},{6,0},{7,1},{8,14},{9,15},{10,... | collective-permute-start | bytes 440 | tf_op jit(solution)/shard_map/ppermute | solution.py:24
  65.0 15.7 %collective-permute-start.6 = (bf16[1,72]{1,0:T(2,128)(2,1)S(1)}, bf16[1,72]{1,0:T(2,128)(2,1)S(1)}, u32[]{:S(2)}, u32[]{:S(2)}) collective-permute-start(bf16[1,72]{1,0:T(2,128)(2,1)S(1)} %get-tuple-element.16), channel_id=1, source_target_pairs={{0,7},{1,6},{2,5},{3,4},{4,3},{5,2},{6,1},{7,0},{8,15},{9,14},{10,... | collective-permute-start | bytes 440 | tf_op jit(solution)/shard_map/ppermute | solution.py:24
  96.9 8.7 %all-to-all-start.1 = ((f32[8,1,72]{2,1,0:T(1,128)}), f32[8,1,72]{2,1,0:T(1,128)S(1)}, u32[]{:S(2)}, u32[]{:S(2)}) async-start(f32[8,1,72]{2,1,0:T(1,128)} %all_to_all.10), calls=%async_computation.1 | async-start | bytes 8192 | tf_op jit(solution)/shard_map/all_to_all | solution.py:83
Sparse Core Ops, SparseCore 0:
  9.9 46.6 all-gather.2
  91.3 42.8 reduce-scatter.3
